TPU v7x, 512 devices: a whole 4x8x8 slice. The times are simulated.
512 devices in a mesh: grp: 16 (over z, core), seq: 32 (over y, x).
Axes of the slice: x: 4, y: 8, z: 8, core: 2. Of those that a mesh axis runs over, the one named last changes fastest.
Arguments:
- hist_keys: bfloat16 [16, 4096, 1024], P('grp', 'seq'), may hold values from -4 to 4
- hist_values: bfloat16 [16, 4096, 1024], P('grp', 'seq'), may hold values from -6 to 6
- latent_queries: bfloat16 [16, 64, 1024], P('grp', 'seq'), may hold values from -48 to 48
- latent_pos: int32 [16, 64], P('grp'), may hold values from 512 to 4095
- targets: int32 [16, 64], P('grp', 'seq'), may hold values from 0 to 127
- out_proj: bfloat16 [1024, 2048], P('seq'), may hold values from -0.1875 to 0.1875
- norm_gain: float32 [2048], replicated, may hold values from 0.1 to 1.9
- unembed: bfloat16 [2048, 128], replicated, may hold values from -0.125 to 0.125
Outputs:
- loss: float32 [16], P('grp')
- grad_queries: bfloat16 [16, 64, 1024], P('grp', 'seq')
- grad_keys: bfloat16 [16, 4096, 1024], P('grp', 'seq')
- grad_values: bfloat16 [16, 4096, 1024], P('grp', 'seq')
- proj_update: float32 [1024, 2048], P('seq')
All inputs are finite; a program needn't handle non-finite values.
Results may differ from a plain program's by a relative error of at most 0.03.
Values may be sent and summed in bfloat16 or wider, within the bound.
A program may use at most 64 MiB of HBM per device.

v0:
```python
import jax
import jax.numpy as jnp
from jax import lax
from jax.sharding import PartitionSpec as P

D = 2048
HD = 128


epsilon = 1e-06
loss_factor = 64.0


def from_everyone(array, axis):
    copies = jnp.broadcast_to(array, (lax.axis_size(axis), *array.shape))
    return lax.all_to_all(copies, axis, split_axis=0, concat_axis=0, tiled=True)


def laid_out(parts, dim):
    parts = jnp.moveaxis(parts, 0, dim)
    dims = parts.shape
    return parts.reshape(*dims[:dim], dims[dim] * dims[dim + 1], *dims[dim + 2 :])


def collect(array, axis, dim):
    parts = from_everyone(array, axis)
    return laid_out(parts, dim)


def sent_together(arrays, axis, split_dim, concat_dim, along):
    both = jnp.concatenate(arrays, axis=along)
    whole, at, done = (
        lax.all_to_all(both, axis, split_axis=split_dim, concat_axis=concat_dim, tiled=True),
        0,
        [],
    )
    for a in arrays:
        done.append(lax.slice_in_dim(whole, at, at + a.shape[along], axis=along))
        at += a.shape[along]
    return tuple(done)


def split_up(array, dim, size):
    before, after = (array.shape[:dim], array.shape[dim + 1 :])
    return jnp.moveaxis(array.reshape(*before, size, -1, *after), dim, 0)


def sent_and_summed(array, axis, dim):
    parts = split_up(array, dim, lax.axis_size(axis))
    arrived = lax.all_to_all(parts, axis, split_axis=0, concat_axis=0, tiled=True)
    return arrived.astype(jnp.float32).sum(axis=0)


def total_of_pieces(array, axis):
    parts = lax.all_gather(array, axis).astype(jnp.float32)
    return parts.sum(axis=0)


def over_copies(array, axis):
    everything = from_everyone(array, axis)
    return jnp.sum(everything, axis=0)


def packed_total(arrays, axis):
    ends = [0]
    for a in arrays:
        ends.append(ends[-1] + a.size)
    total = over_copies(jnp.concatenate([a.ravel() for a in arrays]), axis)
    return tuple((total[b:e].reshape(a.shape) for a, b, e in zip(arrays, ends, ends[1:])))


def repeat_heads(stat):
    return jnp.repeat(stat, HD, axis=-1)


def body(hist_keys, hist_values, latent_queries, latent_pos, targets, out_proj, norm_gain, unembed):
    softmax_scale = HD ** (-0.5)
    seq_keys = hist_keys[0]
    seq_values = hist_values[0]
    position = lax.axis_index("seq")
    tok_rows = seq_keys.shape[0]
    channels = seq_keys.shape[1]
    head_count = channels // HD
    own_rows = latent_queries.shape[1]
    queries = collect(latent_queries[0], "seq", 0)
    latents = queries.shape[0]
    query_heads = queries.reshape(latents, head_count, HD)
    key_heads = seq_keys.reshape(tok_rows, head_count, HD)
    value_heads = seq_values.reshape(tok_rows, head_count, HD)
    places = position * tok_rows + jnp.arange(tok_rows, dtype=jnp.int32)
    visible = (places[None, :] <= latent_pos[0][:, None])[None]
    scores = (
        jnp.einsum("ihd,jhd->hij", query_heads, key_heads, preferred_element_type=jnp.float32)
        * softmax_scale
    )
    largest = jnp.max(jnp.where(visible, scores, -1e30), axis=-1)
    weights = jnp.where(visible, jnp.exp(scores - largest[..., None]), 0.0)
    summed = jnp.sum(weights, axis=-1)
    partial_out = jnp.einsum(
        "hij,jhd->ihd",
        weights.astype(jnp.bfloat16),
        value_heads,
        preferred_element_type=jnp.float32,
    ).reshape(latents, channels)
    pieces = sent_together((largest.T[None], summed.T[None], partial_out[None]), "seq", 1, 0, 2)
    best = jnp.max(pieces[0], axis=0)
    factors = jnp.exp(pieces[0] - best)
    denom = jnp.sum(pieces[1] * factors, axis=0)
    combined = jnp.sum(pieces[2] * repeat_heads(factors), axis=0)
    attn_rows = (combined / repeat_heads(denom)).astype(jnp.bfloat16)
    norm_rows = best + jnp.log(denom)
    attn_all, log_norm = (
        collect(attn_rows.astype(jnp.float32), "seq", 0).astype(attn_rows.dtype),
        collect(norm_rows, "seq", 0),
    )
    slab = out_proj.shape[0]
    attn_cols = lax.dynamic_slice_in_dim(attn_all, position * slab, slab, 1)
    picked = attn_cols
    hidden = sent_and_summed(
        jnp.dot(picked, out_proj, preferred_element_type=jnp.float32).astype(jnp.bfloat16), "seq", 0
    )
    inverse = lax.rsqrt(jnp.mean(hidden * hidden, axis=-1, keepdims=True) + epsilon)
    normed = (hidden * inverse * norm_gain).astype(jnp.bfloat16)
    logits = jnp.dot(normed, unembed, preferred_element_type=jnp.float32)
    log_total = jax.nn.logsumexp(logits, axis=-1, keepdims=True)
    onehot = (jnp.arange(logits.shape[1], dtype=jnp.int32)[None, :] == targets[0][:, None]).astype(
        jnp.float32
    )
    local_loss = jnp.sum(log_total[:, 0] - jnp.sum(logits * onehot, axis=-1))
    grad_logits = (loss_factor * (jnp.exp(logits - log_total) - onehot)).astype(jnp.bfloat16)
    grad_normed = lax.dot_general(
        grad_logits, unembed, (((1,), (1,)), ((), ())), preferred_element_type=jnp.float32
    )
    scaled = norm_gain * grad_normed
    grad_hidden = (
        inverse * scaled - hidden * inverse**3 * jnp.mean(hidden * scaled, axis=-1, keepdims=True)
    ).astype(jnp.bfloat16)
    grad_all = collect(grad_hidden, "seq", 0)
    weight_part = lax.dot_general(
        attn_cols, grad_all, (((0,), (0,)), ((), ())), preferred_element_type=jnp.float32
    )
    grad_cols = lax.dot_general(
        grad_all, out_proj, (((1,), (1,)), ((), ())), preferred_element_type=jnp.float32
    ).astype(jnp.bfloat16)
    grad_attn = collect(grad_cols, "seq", 1)
    grad_heads = grad_attn.reshape(latents, head_count, HD)
    product = grad_attn.astype(jnp.float32) * attn_all.astype(jnp.float32)
    delta = jnp.sum(product.reshape(latents, head_count, HD), axis=-1)
    probs = jnp.where(visible, jnp.exp(scores - log_norm.T[..., None]), 0.0)
    grad_probs = jnp.einsum(
        "ihd,jhd->hij", grad_heads, value_heads, preferred_element_type=jnp.float32
    )
    grad_scores = (probs * (grad_probs - delta.T[..., None])).astype(jnp.bfloat16)
    grad_values = (
        jnp.einsum(
            "hij,ihd->jhd",
            probs.astype(jnp.bfloat16),
            grad_heads,
            preferred_element_type=jnp.float32,
        )
        .reshape(tok_rows, channels)
        .astype(jnp.bfloat16)
    )
    grad_keys = (
        (
            jnp.einsum("hij,ihd->jhd", grad_scores, query_heads, preferred_element_type=jnp.float32)
            * softmax_scale
        )
        .reshape(tok_rows, channels)
        .astype(jnp.bfloat16)
    )
    picked = grad_scores
    terms = jnp.einsum("hij,jhd->ihd", picked, key_heads, preferred_element_type=jnp.float32)
    grad_queries = sent_and_summed(
        (terms.reshape(own_rows * lax.axis_size("seq"), channels) * softmax_scale).astype(
            jnp.bfloat16
        ),
        "seq",
        0,
    ).astype(jnp.bfloat16)
    entries = channels * D
    weight_sum = total_of_pieces(weight_part.astype(jnp.bfloat16), "grp").astype(jnp.float32)
    loss_sum, square_sum = packed_total((local_loss, jnp.sum(weight_sum * weight_sum)), "seq")
    proj_update = weight_sum * lax.rsqrt(square_sum / entries + epsilon)
    return (
        loss_sum.reshape(1),
        grad_queries[None],
        grad_keys[None],
        grad_values[None],
        proj_update,
    )


def solution(mesh):
    placed = (
        P("grp", "seq", None),
        P("grp", "seq", None),
        P("grp", "seq", None),
        P("grp", None),
        P("grp", "seq"),
        P("seq", None),
        P(),
        P(),
    )
    return jax.shard_map(
        body,
        mesh=mesh,
        in_specs=placed,
        out_specs=(
            P("grp"),
            P("grp", "seq", None),
            P("grp", "seq", None),
            P("grp", "seq", None),
            P("seq", None),
        ),
        check_vma=False,
    )
```

profile of v0, /device:TPU:1, one launch (start us, length us, event | category | flops | bytes accessed | tf_op | source)
XLA Modules:
  0.0 172.5 jit_solution(9937094276815897819)
XLA Ops:
  7.2 1.5 broadcast_in_dim.71
  8.7 10.5 %all-to-all-start = ((bf16[32,2,1024]{2,1,0:T(2,128)(2,1)}), bf16[32,2,1024]{2,1,0:T(2,128)(2,1)S(1)}, u32[]{:S(2)}, u32[]{:S(2)}) async-start(bf16[32,2,1024]{2,1,0:T(2,128)(2,1)} %broadcast_in_dim.71), calls=%async_computation | async-start | bytes 262144 | tf_op jit(solution)/shard_map/all_to_all | solution.py:16
  19.2 1.0 copy.105
  20.2 1.0 copy.106
  21.9 6.6 %all-to-all-done = bf16[32,2,1024]{2,1,0:T(2,128)(2,1)S(1)} async-done(((bf16[32,2,1024]{2,1,0:T(2,128)(2,1)}), bf16[32,2,1024]{2,1,0:T(2,128)(2,1)S(1)}, u32[]{:S(2)}, u32[]{:S(2)}) %all-to-all-start) | async-done | bytes 131104 | tf_op jit(solution)/shard_map/all_to_all | solution.py:16
  30.4 14.1 %all_to_all.53 = f32[1,64,1040]{2,0,1:T(1,128)S(1)} all-to-all(f32[1,64,1040]{2,0,1:T(1,128)S(1)} %copy.84), channel_id=1, replica_groups=mesh['grp'=16,'seq'=32] {'seq'}, dimensions={1} | all-to-all | bytes 532480 | tf_op jit(solution)/shard_map/all_to_all | solution.py:33
  47.0 5.0 %all-to-all-start.2 = ((bf16[32,2,1024]{2,1,0:T(2,128)(2,1)}), bf16[32,2,1024]{2,1,0:T(2,128)(2,1)S(1)}, u32[]{:S(2)}, u32[]{:S(2)}) async-start(bf16[32,2,1024]{2,1,0:T(2,128)(2,1)} %broadcast_in_dim.78), calls=%async_computation.2 | async-start | bytes 262144 | tf_op jit(solution)/shard_map/all_to_all | solution.py:16
  52.1 9.4 %all-to-all-done.2 = bf16[32,2,1024]{2,1,0:T(2,128)(2,1)S(1)} async-done(((bf16[32,2,1024]{2,1,0:T(2,128)(2,1)}), bf16[32,2,1024]{2,1,0:T(2,128)(2,1)S(1)}, u32[]{:S(2)}, u32[]{:S(2)}) %all-to-all-start.2) | async-done | bytes 131104 | tf_op jit(solution)/shard_map/all_to_all | solution.py:16
  62.0 13.5 %all_to_all.54 = bf16[32,2,2048]{2,1,0:T(2,128)(2,1)S(1)} all-to-all(bf16[32,2,2048]{2,1,0:T(2,128)(2,1)S(1)} %reshape.159), channel_id=1, replica_groups=mesh['grp'=16,'seq'=32] {'seq'}, dimensions={0} | all-to-all | bytes 524288 | tf_op jit(solution)/shard_map/all_to_all | solution.py:50
  77.8 13.9 %all_to_all.55 = bf16[32,2,2048]{2,1,0:T(2,128)(2,1)S(1)} all-to-all(bf16[32,2,2048]{2,1,0:T(2,128)(2,1)S(1)} %broadcast_in_dim.79), channel_id=1, replica_groups=mesh['grp'=16,'seq'=32] {'seq'}, dimensions={0} | all-to-all | bytes 524288 | tf_op jit(solution)/shard_map/all_to_all | solution.py:16
  91.7 0.9 convolution_convert_fusion.1
  93.3 3.9 %all-to-all-start.6 = ((f32[32,2,8]{2,1,0:T(2,128)}), f32[32,2,8]{2,1,0:T(2,128)S(1)}, u32[]{:S(2)}, u32[]{:S(2)}) async-start(f32[32,2,8]{2,1,0:T(2,128)} %broadcast_in_dim.81), calls=%async_computation.6 | async-start | bytes 65536 | tf_op jit(solution)/shard_map/all_to_all | solution.py:16
  97.4 0.8 reshape.168
  98.3 7.5 %all-to-all-done.6 = f32[32,2,8]{2,1,0:T(2,128)S(1)} async-done(((f32[32,2,8]{2,1,0:T(2,128)}), f32[32,2,8]{2,1,0:T(2,128)S(1)}, u32[]{:S(2)}, u32[]{:S(2)}) %all-to-all-start.6) | async-done | bytes 2080 | tf_op jit(solution)/shard_map/all_to_all | solution.py:16
  105.8 3.9 %all-to-all-start.7 = ((bf16[32,2,1024]{2,1,0:T(2,128)(2,1)}), bf16[32,2,1024]{2,1,0:T(2,128)(2,1)S(1)}, u32[]{:S(2)}, u32[]{:S(2)}) async-start(bf16[32,2,1024]{2,1,0:T(2,128)(2,1)} %reshape.168), calls=%async_computation.7 | async-start | bytes 262144 | tf_op jit(solution)/shard_map/all_to_all | solution.py:16
  110.0 9.1 %all-to-all-done.7 = bf16[32,2,1024]{2,1,0:T(2,128)(2,1)S(1)} async-done(((bf16[32,2,1024]{2,1,0:T(2,128)(2,1)}), bf16[32,2,1024]{2,1,0:T(2,128)(2,1)S(1)}, u32[]{:S(2)}, u32[]{:S(2)}) %all-to-all-start.7) | async-done | bytes 131104 | tf_op jit(solution)/shard_map/all_to_all | solution.py:16
  121.9 3.9 %all-to-all-start.8 = ((bf16[32,2,1024]{2,1,0:T(2,128)(2,1)}), bf16[32,2,1024]{2,1,0:T(2,128)(2,1)S(1)}, u32[]{:S(2)}, u32[]{:S(2)}) async-start(bf16[32,2,1024]{2,1,0:T(2,128)(2,1)} %convert_element_type.128), calls=%async_computation.8 | async-start | bytes 262144 | tf_op jit(solution)/shard_map/all_to_all | solution.py:50
  126.1 14.7 %all-gather.3.cloned.1.call-done = bf16[512,2048]{1,0:T(8,128)(2,1)} async-done(((bf16[32,2048]{1,0:T(8,128)(2,1)}), bf16[512,2048]{1,0:T(8,128)(2,1)}) %all-gather.3.cloned.1.call-update) | async-done | bytes 2097168 | tf_op jit(solution)/shard_map/all_gather | solution.py:55
  140.8 2.0 %convert_reduce_fusion = f32[32,2048]{1,0:T(8,128)S(1)} fusion(bf16[16,32,2048]{2,1,0:T(8,128)(2,1)} %bitcast.69), kind=kLoop, calls=%fused_computation | loop fusion | flops 2031616 | bytes 2359296 | tf_op jit(solution)/shard_map/reduce_sum | solution.py:56
  143.5 1.4 pad_maximum_fusion
  145.5 9.6 %all-to-all-start.5 = ((f32[32,1,2]{2,1,0:T(1,128)}), f32[32,1,2]{2,1,0:T(1,128)S(1)}, u32[]{:S(2)}, u32[]{:S(2)}) async-start(f32[32,1,2]{2,1,0:T(1,128)} %broadcast_in_dim.80), calls=%async_computation.5 | async-start | bytes 32768 | tf_op jit(solution)/shard_map/all_to_all | solution.py:16
  155.3 0.9 copy.97
  156.2 0.8 copy.96
  157.8 5.8 %all-to-all-done.5 = f32[32,1,2]{2,1,0:T(1,128)S(1)} async-done(((f32[32,1,2]{2,1,0:T(1,128)}), f32[32,1,2]{2,1,0:T(1,128)S(1)}, u32[]{:S(2)}, u32[]{:S(2)}) %all-to-all-start.5) | async-done | bytes 288 | tf_op jit(solution)/shard_map/all_to_all | solution.py:16
  (71 shorter events, 15.8 us)
Async XLA Ops:
  7.2 68.7 %copy-start = (bf16[2048,128]{1,0:T(8,128)(2,1)S(1)}, bf16[2048,128]{1,0:T(8,128)(2,1)}, u32[]{:S(2)}) copy-start(bf16[2048,128]{1,0:T(8,128)(2,1)} %param.15) | copy-start | bytes 1572868
  8.7 19.9 %all-to-all-start = ((bf16[32,2,1024]{2,1,0:T(2,128)(2,1)}), bf16[32,2,1024]{2,1,0:T(2,128)(2,1)S(1)}, u32[]{:S(2)}, u32[]{:S(2)}) async-start(bf16[32,2,1024]{2,1,0:T(2,128)(2,1)} %broadcast_in_dim.71), calls=%async_computation | async-start | bytes 262144 | tf_op jit(solution)/shard_map/all_to_all | solution.py:16
  30.4 31.1 %copy-start.1 = (bf16[32,2048]{1,0:T(8,128)(2,1)S(1)}, bf16[32,2048]{1,0:T(8,128)(2,1)}, u32[]{:S(2)}) copy-start(bf16[32,2048]{1,0:T(8,128)(2,1)} %param.13) | copy-start | bytes 393220
  45.4 30.5 %copy-start.3 = (f32[2048]{0:T(1024)S(1)}, f32[2048]{0:T(1024)}, u32[]{:S(2)}) copy-start(f32[2048]{0:T(1024)} %param.14) | copy-start | bytes 24580
  45.8 30.5 %copy-start.2 = (s32[1,2]{1,0:T(1,128)S(1)}, s32[1,2]{1,0:T(1,128)}, u32[]{:S(2)}) copy-start(s32[1,2]{1,0:T(1,128)} %param.12) | copy-start | bytes 28
  47.0 14.4 %all-to-all-start.2 = ((bf16[32,2,1024]{2,1,0:T(2,128)(2,1)}), bf16[32,2,1024]{2,1,0:T(2,128)(2,1)S(1)}, u32[]{:S(2)}, u32[]{:S(2)}) async-start(bf16[32,2,1024]{2,1,0:T(2,128)(2,1)} %broadcast_in_dim.78), calls=%async_computation.2 | async-start | bytes 262144 | tf_op jit(solution)/shard_map/all_to_all | solution.py:16
  52.0 88.8 %all-gather.3.cloned.1.call-start = ((), (), s32[]{:S(2)}) async-start(), calls=%async_computation.9 | async-start | bytes 2228224 | tf_op jit(solution)/shard_map/all_gather | solution.py:55
  93.3 12.5 %all-to-all-start.6 = ((f32[32,2,8]{2,1,0:T(2,128)}), f32[32,2,8]{2,1,0:T(2,128)S(1)}, u32[]{:S(2)}, u32[]{:S(2)}) async-start(f32[32,2,8]{2,1,0:T(2,128)} %broadcast_in_dim.81), calls=%async_computation.6 | async-start | bytes 65536 | tf_op jit(solution)/shard_map/all_to_all | solution.py:16
  105.8 13.3 %all-to-all-start.7 = ((bf16[32,2,1024]{2,1,0:T(2,128)(2,1)}), bf16[32,2,1024]{2,1,0:T(2,128)(2,1)S(1)}, u32[]{:S(2)}, u32[]{:S(2)}) async-start(bf16[32,2,1024]{2,1,0:T(2,128)(2,1)} %reshape.168), calls=%async_computation.7 | async-start | bytes 262144 | tf_op jit(solution)/shard_map/all_to_all | solution.py:16
  121.9 22.9 %all-to-all-start.8 = ((bf16[32,2,1024]{2,1,0:T(2,128)(2,1)}), bf16[32,2,1024]{2,1,0:T(2,128)(2,1)S(1)}, u32[]{:S(2)}, u32[]{:S(2)}) async-start(bf16[32,2,1024]{2,1,0:T(2,128)(2,1)} %convert_element_type.128), calls=%async_computation.8 | async-start | bytes 262144 | tf_op jit(solution)/shard_map/all_to_all | solution.py:50
  145.5 18.1 %all-to-all-start.5 = ((f32[32,1,2]{2,1,0:T(1,128)}), f32[32,1,2]{2,1,0:T(1,128)S(1)}, u32[]{:S(2)}, u32[]{:S(2)}) async-start(f32[32,1,2]{2,1,0:T(1,128)} %broadcast_in_dim.80), calls=%async_computation.5 | async-start | bytes 32768 | tf_op jit(solution)/shard_map/all_to_all | solution.py:16
Sparse Core Ops, SparseCore 0:
  92.8 47.9 all-gather.2
where the time goes:
time: 173 us; the launch traced here: 172 us
  waiting for transfers between devices  53.1 us (31%)
  blocking collectives  41.5 us (24%)
  starting transfers between devices  36.7 us (21%)
  between operations  15.1 us (9%)
  local copies, waits for them, and re-layouts  12.7 us (7%)
  other arithmetic  9.4 us (5%)
  matrix products  3.89 us (2%)
    all_to_all x5, waiting for transfers between devices, from_everyone(): return lax.all_to_all(copies, axis, split_axis=0, concat_axis=0, tiled=True)  38.4 us
    all_to_all x5, starting transfers between devices, from_everyone(): return lax.all_to_all(copies, axis, split_axis=0, concat_axis=0, tiled=True)  32.8 us
    all_gather x1, waiting for transfers between devices, total_of_pieces(): parts = lax.all_gather(array, axis).astype(jnp.float32)  14.7 us
    all_to_all x1, blocking collectives, sent_together(): lax.all_to_all(both, axis, split_axis=split_dim, concat_axis=concat_dim,...  14.1 us
    all_to_all x1, blocking collectives, from_everyone(): return lax.all_to_all(copies, axis, split_axis=0, concat_axis=0, tiled=True)  13.9 us
    all_to_all x1, blocking collectives, sent_and_summed(): lax.all_to_all(parts, axis, split_axis=0, concat_axis=0, tiled=True)  13.5 us
    unnamed x16, local copies, waits for them, and re-layouts  4.91 us
    all_to_all x1, starting transfers between devices, sent_and_summed(): lax.all_to_all(parts, axis, split_axis=0, concat_axis=0, tiled=True)  3.86 us
  transfers between devices with their start and end apart: 7, of which 6 were waited for; matrix products, arithmetic and copies ran while one was open for 8% of the time, Pallas kernels for 0%

commit v1 on v0

v1 whole, which is shorter than its diff:
```python
import functools

import jax
import jax.numpy as jnp
from jax import lax
from jax.experimental import pallas as pl
from jax.experimental.pallas import tpu as pltpu
from jax.sharding import PartitionSpec as P

MESH = pl.DeviceIdType.MESH
BF = jnp.bfloat16
F32 = jnp.float32

D = 2048
HD = 128
HEADS = 8
NL = 64
TOK = 128
HC = 1024
NS = 32
NG = 16
NX = 4
NY = 8
SLABS = 16
EPS = 1e-06
LOSS_FACTOR = 64.0
SCALE = HD ** (-0.5)

RANGE_T = ((1,), (1,))


def dot(a, b, dims=((1,), (0,))):
    return lax.dot_general(a, b, (dims, ((), ())), preferred_element_type=F32)


def iota(shape, dim):
    return lax.broadcasted_iota(jnp.int32, shape, dim)


def column_to_row(col, rows):
    wide = jnp.broadcast_to(col, (rows, 128))
    picked = jnp.where(iota((rows, 128), 0) == iota((rows, 128), 1), wide, 0.0)
    return jnp.sum(picked, axis=0, keepdims=True)


def row_to_column(row, rows):
    wide = jnp.broadcast_to(row, (rows, 128))
    picked = jnp.where(iota((rows, 128), 0) == iota((rows, 128), 1), wide, 0.0)
    return jnp.sum(picked, axis=1, keepdims=True)


def wait_bytes(ref, sem):
    pltpu.make_async_copy(ref, ref, sem).wait()


def kernel(
    k_ref, v_ref, q_ref, pos_ref, tgt_ref, w_ref, gain_row_ref, gain_ref, u_ref,
    loss_ref, gq_ref, gk_ref, gv_ref, gw_ref,
    qsend, qbuf, wbuf, wusend, wubuf, osend, obuf, stsend, stbuf, asend, abuf, lsend, lbuf,
    ysend, ybuf, sssend, ssbuf, dsend, dbuf, gqsend, gqbuf, gsend, gbuf, tsend, tbuf,
    s1send, s1buf, s2send, s2buf,
    flat, flat2, sc, awide, lse_s, tgt_s, own_s, kap_s, st_s,
    ssem, rsem,
):
    g = lax.axis_index("grp")
    d = lax.axis_index("seq")
    y, x = d // NX, d % NX
    slab, par = d // 2, d % 2
    owner = 16 * par + g

    def seq_peer(i):
        return lax.rem(d + i, NS)

    def grp_peer(i):
        return lax.rem(g + i, NG)

    barrier = pltpu.get_barrier_semaphore()

    def greet_seq(i, c):
        pl.semaphore_signal(barrier, inc=1, device_id={"grp": g, "seq": seq_peer(i)}, device_id_type=MESH)
        return c

    def greet_grp(i, c):
        pl.semaphore_signal(barrier, inc=1, device_id={"grp": grp_peer(i), "seq": d}, device_id_type=MESH)
        return c

    def greet_tiles(i, c):
        gs, ds = d % 16, 2 * i + d // 16

        @pl.when(jnp.logical_or(gs != g, ds != d))
        def _():
            pl.semaphore_signal(barrier, inc=1, device_id={"grp": gs, "seq": ds}, device_id_type=MESH)

        return c

    lax.fori_loop(1, NS, greet_seq, 0)
    lax.fori_loop(1, NG, greet_grp, 0)
    lax.fori_loop(0, SLABS, greet_tiles, 0)

    def to_seq(src, dst, n):
        def one(i, c):
            t = seq_peer(i)
            pltpu.make_async_remote_copy(
                src_ref=src(t), dst_ref=dst, send_sem=ssem.at[n], recv_sem=rsem.at[n],
                device_id={"grp": g, "seq": t}, device_id_type=MESH,
            ).start()
            return c

        lax.fori_loop(1, NS, one, 0)

    def to_grp(src, dst, n):
        def one(i, c):
            t = grp_peer(i)
            pltpu.make_async_remote_copy(
                src_ref=src(t), dst_ref=dst, send_sem=ssem.at[n], recv_sem=rsem.at[n],
                device_id={"grp": t, "seq": d}, device_id_type=MESH,
            ).start()
            return c

        lax.fori_loop(1, NG, one, 0)

    q32 = q_ref[...].astype(F32)
    for h in range(HEADS):
        own_s[pl.ds(h, 2, stride=8), :] = q32[:, h * HD : (h + 1) * HD]
    qsend[...] = own_s[...].astype(BF)
    qbuf[d] = own_s[...].astype(BF)
    pos = row_to_column(pos_ref[...].astype(F32), NL)
    places = (d * TOK + iota((NL, TOK), 1)).astype(F32)
    visible = places <= pos
    wg = w_ref[...].astype(F32) * gain_row_ref[...]
    wg_high = wg.astype(BF)
    wg_low = (wg - wg_high.astype(F32)).astype(BF)
    wu_own = (dot(wg_high, u_ref[...]) + dot(wg_low, u_ref[...])).astype(BF)
    wusend[...] = wu_own
    wubuf[d] = wu_own
    wbuf[d] = w_ref[:, pl.ds(pl.multiple_of(slab * 128, 128), 128)]

    tiles_out = jnp.where(owner == d, NG - 1, NG)
    pl.semaphore_wait(barrier, NS - 1 + NG - 1 + tiles_out)

    to_seq(lambda t: qsend, qbuf.at[d], 0)
    to_seq(lambda t: w_ref.at[:, pl.ds(pl.multiple_of((t // 2) * 128, 128), 128)], wbuf.at[d], 1)

    wait_bytes(qbuf.at[pl.ds(0, NS - 1)], rsem.at[0])
    flat[...] = qbuf[...].reshape(NL * HEADS, HD).astype(F32)
    lanes = iota((NL, 128), 1)
    ms = jnp.zeros((NL, 128), F32)
    ls = jnp.zeros((NL, 128), F32)
    for h in range(HEADS):
        cols = slice(h * HD, (h + 1) * HD)
        qh = flat[pl.ds(h, NL, stride=8), :].astype(BF)
        s = dot(qh, k_ref[:, cols], RANGE_T) * SCALE
        sc[h] = s
        m = jnp.max(jnp.where(visible, s, -1e30), axis=-1, keepdims=True)
        p = jnp.where(visible, jnp.exp(s - m), 0.0)
        ms = jnp.where(lanes == h, m, ms)
        ls = jnp.where(lanes == h, jnp.sum(p, axis=-1, keepdims=True), ls)
        flat2[pl.ds(h, NL, stride=8), :] = dot(p.astype(BF), v_ref[:, cols])
    o_all = flat2[...].reshape(NS, 16, HD).astype(BF)
    osend[...] = o_all
    st_s[0] = ms
    st_s[1] = ls
    stsend[:, 0, :] = st_s[0, pl.ds(0, NS, stride=2), :]
    stsend[:, 1, :] = st_s[0, pl.ds(1, NS, stride=2), :]
    stsend[:, 2, :] = st_s[1, pl.ds(0, NS, stride=2), :]
    stsend[:, 3, :] = st_s[1, pl.ds(1, NS, stride=2), :]
    to_seq(lambda t: stsend.at[t], stbuf.at[d], 3)
    to_seq(lambda t: osend.at[t], obuf.at[d], 2)
    to_seq(lambda t: wusend, wubuf.at[d], 4)
    stbuf[d] = stsend[d]
    obuf[d] = osend[d]

    wait_bytes(stbuf.at[pl.ds(0, NS - 1)], rsem.at[3])
    weights = []
    head_lane = iota((1, 128), 1)
    for r in range(2):
        mr = stbuf[:, r, :]
        lr = stbuf[:, 2 + r, :]
        best = jnp.max(mr, axis=0, keepdims=True)
        f = jnp.exp(mr - best)
        denom = jnp.sum(lr * f, axis=0, keepdims=True)
        denom = jnp.where(head_lane < HEADS, denom, 1.0)
        weights.append(jnp.transpose(f / denom)[0:HEADS, :])
        row = jnp.where(head_lane < HEADS, best + jnp.log(denom), tgt_ref[0, r].astype(F32))
        lsend[r : r + 1, :] = row
    wait_bytes(obuf.at[pl.ds(0, NS - 1)], rsem.at[2])
    w8 = jnp.concatenate(weights, axis=0)
    total = jnp.zeros((16, HD), F32)
    for b in range(NS):
        total = total + w8[:, b : b + 1] * obuf[b].astype(F32)
    attn_own = total.astype(BF)
    asend[...] = attn_own
    abuf[d] = attn_own
    lbuf[d] = lsend[...]
    to_seq(lambda t: asend, abuf.at[d], 5)
    to_seq(lambda t: lsend, lbuf.at[d], 6)

    wait_bytes(wbuf.at[pl.ds(0, NS - 1)], rsem.at[1])
    wait_bytes(wubuf.at[pl.ds(0, NS - 1)], rsem.at[4])
    wc = wbuf[...].reshape(HC, 128)
    wu = wubuf[...].reshape(HC, 128)
    wait_bytes(abuf.at[pl.ds(0, NS - 1)], rsem.at[5])
    flat2[...] = abuf[...].reshape(NL * HEADS, HD).astype(F32)
    for h in range(HEADS):
        awide[:, h * HD : (h + 1) * HD] = flat2[pl.ds(h, NL, stride=8), :].astype(BF)
    a = awide[...]
    xs = dot(a, wc)
    ss_row = column_to_row(jnp.sum(xs * xs, axis=-1, keepdims=True), NL)
    sssend[...] = ss_row
    ssbuf[slab] = ss_row

    def near_peers(src, dst, n):
        def one(i, c):
            tx = jnp.where(i % 2 == 0, x, NX - 1 - x)
            t = lax.rem(y + i // 2, NY) * NX + tx
            pltpu.make_async_remote_copy(
                src_ref=src(t), dst_ref=dst, send_sem=ssem.at[n], recv_sem=rsem.at[n],
                device_id={"grp": g, "seq": t}, device_id_type=MESH,
            ).start()
            return c

        lax.fori_loop(1, SLABS, one, 0)

    near_peers(lambda t: sssend, ssbuf.at[slab], 7)
    xb = xs.astype(BF)
    for h in range(HEADS):
        flat2[pl.ds(h, NL, stride=8), :] = dot(xb, wc[h * HD : (h + 1) * HD, :], RANGE_T)
    ysend[...] = flat2[...].reshape(NS, 16, HD).astype(BF)
    near_peers(lambda t: ysend.at[t], ybuf.at[slab], 8)
    ybuf[slab] = ysend[d]
    raw = dot(a, wu)

    wait_bytes(lbuf.at[pl.ds(0, NS - 1)], rsem.at[6])
    for r in range(2):
        lb = lbuf[:, r, :]
        for h in range(HEADS):
            lse_s[h, pl.ds(r, NS, stride=2), :] = jnp.broadcast_to(lb[:, h : h + 1], (NS, 128))
        tgt_s[pl.ds(r, NS, stride=2), :] = jnp.broadcast_to(lb[:, HEADS : HEADS + 1], (NS, 128))
    onehot = (lanes.astype(F32) == tgt_s[...]).astype(F32)

    wait_bytes(ssbuf.at[pl.ds(0, SLABS - 1)], rsem.at[7])
    square = row_to_column(jnp.sum(ssbuf[:, 0, :], axis=0, keepdims=True), NL)
    inverse = lax.rsqrt(square * (1.0 / D) + EPS)
    logits = raw * inverse
    top = jnp.max(logits, axis=-1, keepdims=True)
    log_total = top + jnp.log(jnp.sum(jnp.exp(logits - top), axis=-1, keepdims=True))
    per_latent = log_total - jnp.sum(logits * onehot, axis=-1, keepdims=True)
    loss_ref[...] = jnp.sum(per_latent, axis=0, keepdims=True)
    dl = (LOSS_FACTOR * (jnp.exp(logits - log_total) - onehot)).astype(BF)
    mean_xg = jnp.sum(dl.astype(F32) * raw, axis=-1, keepdims=True) * (1.0 / D)
    kappa = inverse * inverse * inverse * mean_xg
    kap_s[...] = jnp.broadcast_to(kappa, (NL, 128))

    u_slab = u_ref[pl.ds(pl.multiple_of(slab * 128, 128), 128), :]
    dn = dot(dl, u_slab, RANGE_T)
    dx = (inverse * gain_ref[pl.ds(slab, 1), :] * dn - kappa * xs).astype(BF)
    a_half = awide[:, pl.ds(pl.multiple_of(par * 512, 512), 512)]
    gpart = dot(a_half, dx, ((0,), (0,)))
    gsend[...] = gpart.reshape(NG, 32, 128).astype(BF)
    to_grp(lambda t: gsend.at[t], gbuf.at[g], 9)
    gbuf[g] = gsend[g]

    for h in range(HEADS):
        flat2[pl.ds(h, NL, stride=8), :] = dot(dl, wu[h * HD : (h + 1) * HD, :], RANGE_T) * inverse
    wait_bytes(ybuf.at[pl.ds(0, SLABS - 1)], rsem.at[8])
    ysum = jnp.sum(ybuf[...].astype(F32), axis=0)
    k2 = jnp.concatenate(
        [jnp.broadcast_to(kap_s[pl.ds(2 * d + r, 1), :], (HEADS, 128)) for r in range(2)], axis=0
    )
    dattn_own = (flat2[pl.ds(pl.multiple_of(d * 16, 16), 16), :] - k2 * ysum).astype(BF)
    dsend[...] = dattn_own
    dbuf[d] = dattn_own
    to_seq(lambda t: dsend, dbuf.at[d], 10)

    wait_bytes(dbuf.at[pl.ds(0, NS - 1)], rsem.at[10])
    flat2[...] = dbuf[...].reshape(NL * HEADS, HD).astype(F32)
    kept = []
    for h in range(HEADS):
        cols = slice(h * HD, (h + 1) * HD)
        d32 = flat2[pl.ds(h, NL, stride=8), :]
        dh = d32.astype(BF)
        delta = jnp.sum(d32 * awide[:, cols].astype(F32), axis=-1, keepdims=True)
        probs = jnp.where(visible, jnp.exp(sc[h] - lse_s[h]), 0.0)
        dp = dot(dh, v_ref[:, cols], RANGE_T)
        ds = (probs * (dp - delta)).astype(BF)
        kept.append((probs.astype(BF), ds, dh))
    for h in range(HEADS):
        cols = slice(h * HD, (h + 1) * HD)
        flat2[pl.ds(h, NL, stride=8), :] = dot(kept[h][1], k_ref[:, cols]) * SCALE
    gqsend[...] = flat2[...].reshape(NS, 16, HD).astype(BF)
    to_seq(lambda t: gqsend.at[t], gqbuf.at[d], 11)
    gqbuf[d] = gqsend[d]

    wait_bytes(gbuf.at[pl.ds(0, NG - 1)], rsem.at[9])
    tile = jnp.sum(gbuf[...].astype(F32), axis=0)
    squares = jnp.sum(jnp.sum(tile * tile, axis=0, keepdims=True), axis=1, keepdims=True)
    s1 = jnp.broadcast_to(squares, (1, 128))
    s1send[...] = s1
    s1buf[d] = s1
    to_seq(lambda t: s1send, s1buf.at[d], 12)
    tsend[...] = tile.astype(BF)

    def one_owner(i, c):
        @pl.when(jnp.logical_or(i > 0, owner != d))
        def _():
            pltpu.make_async_remote_copy(
                src_ref=tsend, dst_ref=tbuf.at[slab], send_sem=ssem.at[13], recv_sem=rsem.at[13],
                device_id={"grp": grp_peer(i), "seq": owner}, device_id_type=MESH,
            ).start()

        return c

    lax.fori_loop(0, NG, one_owner, 0)

    @pl.when(owner == d)
    def _():
        tbuf[slab] = tsend[...]

    for h in range(HEADS):
        cols = slice(h * HD, (h + 1) * HD)
        pr, ds, dh = kept[h]
        gv_ref[:, cols] = dot(pr, dh, ((0,), (0,))).astype(BF)
        qh = flat[pl.ds(h, NL, stride=8), :].astype(BF)
        gk_ref[:, cols] = (dot(ds, qh, ((0,), (0,))) * SCALE).astype(BF)

    wait_bytes(s1buf.at[pl.ds(0, NS - 1)], rsem.at[12])
    s2 = jnp.sum(s1buf[:, 0, :], axis=0, keepdims=True)
    s2send[...] = s2
    s2buf[g] = s2
    to_grp(lambda t: s2send, s2buf.at[g], 14)

    wait_bytes(gqbuf.at[pl.ds(0, NS - 1)], rsem.at[11])
    own_s[...] = jnp.sum(gqbuf[...].astype(F32), axis=0)
    for h in range(HEADS):
        gq_ref[:, h * HD : (h + 1) * HD] = own_s[pl.ds(h, 2, stride=8), :].astype(BF)

    @pl.when(owner == d)
    def _():
        wait_bytes(tbuf.at[pl.ds(0, SLABS - 1)], rsem.at[13])
        wait_bytes(tbuf.at[pl.ds(0, NG - 1)], ssem.at[13])

    @pl.when(owner != d)
    def _():
        wait_bytes(tbuf, rsem.at[13])
        wait_bytes(tbuf, ssem.at[13])

    wait_bytes(s2buf.at[pl.ds(0, NG - 1)], rsem.at[14])
    total_squares = jnp.sum(s2buf[:, 0, :], axis=0, keepdims=True)
    factor = lax.rsqrt(total_squares * (1.0 / (HC * D)) + EPS)
    for j in range(SLABS):
        gw_ref[:, j * 128 : (j + 1) * 128] = tbuf[j].astype(F32) * factor

    for n, ref, count in (
        (0, qbuf, NS - 1), (1, wbuf, NS - 1), (2, obuf, NS - 1), (3, stbuf, NS - 1), (4, wubuf, NS - 1),
        (5, abuf, NS - 1), (6, lbuf, NS - 1), (7, ssbuf, SLABS - 1), (8, ybuf, SLABS - 1), (9, gbuf, NG - 1),
        (10, dbuf, NS - 1), (11, gqbuf, NS - 1), (12, s1buf, NS - 1), (14, s2buf, NG - 1),
    ):
        wait_bytes(ref.at[pl.ds(0, count)], ssem.at[n])


def body(hist_keys, hist_values, latent_queries, latent_pos, targets, out_proj, norm_gain, unembed):
    vmem = pl.BlockSpec(memory_space=pltpu.VMEM)
    smem = pl.BlockSpec(memory_space=pltpu.SMEM)
    pos = jnp.pad(latent_pos, ((0, 0), (0, 128 - NL)))
    rows16 = lambda n: pltpu.VMEM((n, 16, 128), BF)
    rows32 = lambda n: pltpu.VMEM((n, 32, 128), BF)
    loss, gq, gk, gv, gw = pl.pallas_call(
        kernel,
        out_shape=(
            jax.ShapeDtypeStruct((1, 1), F32),
            jax.ShapeDtypeStruct((2, HC), BF),
            jax.ShapeDtypeStruct((TOK, HC), BF),
            jax.ShapeDtypeStruct((TOK, HC), BF),
            jax.ShapeDtypeStruct((32, D), F32),
        ),
        in_specs=[vmem, vmem, vmem, vmem, smem, vmem, vmem, vmem, vmem],
        out_specs=(vmem,) * 5,
        scratch_shapes=[
            pltpu.VMEM((16, 128), BF), rows16(NS),
            rows32(NS), pltpu.VMEM((32, 128), BF), rows32(NS),
            rows16(NS), rows16(NS),
            pltpu.VMEM((NS, 4, 128), F32), pltpu.VMEM((NS, 4, 128), F32),
            pltpu.VMEM((16, 128), BF), rows16(NS),
            pltpu.VMEM((2, 128), F32), pltpu.VMEM((NS, 2, 128), F32),
            rows16(NS), rows16(SLABS),
            pltpu.VMEM((1, 128), F32), pltpu.VMEM((SLABS, 1, 128), F32),
            pltpu.VMEM((16, 128), BF), rows16(NS),
            rows16(NS), rows16(NS),
            rows32(NG), rows32(NG),
            pltpu.VMEM((32, 128), BF), rows32(SLABS),
            pltpu.VMEM((1, 128), F32), pltpu.VMEM((NS, 1, 128), F32),
            pltpu.VMEM((1, 128), F32), pltpu.VMEM((NG, 1, 128), F32),
            pltpu.VMEM((NL * HEADS, 128), F32), pltpu.VMEM((NL * HEADS, 128), F32),
            pltpu.VMEM((HEADS, NL, TOK), F32),
            pltpu.VMEM((NL, HC), BF),
            pltpu.VMEM((HEADS, NL, 128), F32), pltpu.VMEM((NL, 128), F32),
            pltpu.VMEM((16, 128), F32), pltpu.VMEM((NL, 128), F32),
            pltpu.VMEM((2, NL, 128), F32),
            pltpu.SemaphoreType.DMA((15,)), pltpu.SemaphoreType.DMA((15,)),
        ],
        compiler_params=pltpu.CompilerParams(
            collective_id=0, has_side_effects=True, vmem_limit_bytes=32 << 20
        ),
    )(
        hist_keys[0], hist_values[0], latent_queries[0], pos, targets, out_proj,
        norm_gain.reshape(1, D), norm_gain.reshape(SLABS, 128), unembed,
    )
    return loss.reshape(1), gq[None], gk[None], gv[None], gw


def solution(mesh):
    placed = (
        P("grp", "seq", None), P("grp", "seq", None), P("grp", "seq", None), P("grp", None),
        P("grp", "seq"), P("seq", None), P(), P(),
    )
    return jax.shard_map(
        body,
        mesh=mesh,
        in_specs=placed,
        out_specs=(
            P("grp"), P("grp", "seq", None), P("grp", "seq", None), P("grp", "seq", None), P("seq", None),
        ),
        check_vma=False,
    )
```

time: 173 us -> 91.6 us (0.53)
  Pallas kernels: 0 us -> 80.3 us
  waiting for transfers between devices: 53.1 us -> 0 us
  blocking collectives: 41.5 us -> 0 us
  starting transfers between devices: 36.7 us -> 0 us
  between operations: 15.1 us -> 2.47 us
  other arithmetic: 9.4 us -> 0 us
  local copies, waits for them, and re-layouts: 12.7 us -> 8.54 us
  matrix products: 3.89 us -> 0 us
    pallas_call x0 -> x1, Pallas kernels: none -> 80.3 us  [body(): pl.pallas_call(kernel, out_shape=(jax.ShapeDtypeStruct((1, 1), F32), jax....]
    all_to_all x3 -> x0, blocking collectives: 41.5 us -> none  [the longest x1 14.1 us: sent_together(): lax.all_to_all(both, axis, split_axis=split_dim, concat_axis=concat_dim,...]
    all_to_all x6 -> x0, waiting for transfers between devices: 38.4 us -> none  [the longest x5 38.4 us: from_everyone(): return lax.all_to_all(copies, axis, split_axis=0, concat_axis=0, tiled=True)]
    all_to_all x6 -> x0, starting transfers between devices: 36.6 us -> none  [the longest x5 32.8 us: from_everyone(): return lax.all_to_all(copies, axis, split_axis=0, concat_axis=0, tiled=True)]
    all_gather x1 -> x0, waiting for transfers between devices: 14.7 us -> none  [total_of_pieces(): parts = lax.all_gather(array, axis).astype(jnp.float32)]
    reduce_sum x13 -> x0, other arithmetic: 5.72 us -> none  [the longest x1 1.99 us: total_of_pieces(): return parts.sum(axis=0)]
    dot_general x11 -> x0, matrix products: 3.89 us -> none  [the longest x1 0.95 us: body(): lax.dot_general(attn_cols, grad_all, (((0,), (0,)), ((), ())), preferred_...]
    broadcast_in_dim x8 -> x0, local copies, waits for them, and re-layouts: 3.87 us -> none  [the longest x5 3.57 us: from_everyone(): copies = jnp.broadcast_to(array, (lax.axis_size(axis), *array.shape))]
  transfers between devices with their start and end apart: 7 -> 0, of which waited for: 6 -> 0; matrix products, arithmetic and copies ran while one was open for 8% -> 0% of each run, Pallas kernels for 0% -> 0%
where the time goes in v1:
time: 91.6 us; the launch traced here: 91.3 us
  Pallas kernels  80.3 us (88%)
  local copies, waits for them, and re-layouts  8.54 us (9%)
  between operations  2.47 us (3%)
    pallas_call x1, Pallas kernels, body(): pl.pallas_call(kernel, out_shape=(jax.ShapeDtypeStruct((1, 1), F32), jax....  80.3 us
    unnamed x20, local copies, waits for them, and re-layouts  8.54 us

profile of v1, /device:TPU:1, one launch (start us, length us, event | category | flops | bytes accessed | tf_op | source)
XLA Modules:
  0.0 91.3 jit_solution(18232359841373921580)
XLA Ops:
  0.6 0.0 copy-start.4
  0.6 0.0 copy-start.7
  0.7 0.7 copy-done.7
  1.3 0.0 copy-start.6
  1.3 0.0 copy-done.4
  1.3 0.6 copy-done.6
  2.0 0.0 copy-start
  2.0 1.0 %copy-done = bf16[2048,128]{1,0:T(8,128)(2,1)S(1)} copy-done((bf16[2048,128]{1,0:T(8,128)(2,1)S(1)}, bf16[2048,128]{1,0:T(8,128)(2,1)}, u32[]{:S(2)}) %copy-start) | copy-done | bytes 524312
  3.0 0.0 copy-start.1
  3.0 0.9 %copy-done.1 = bf16[1,128,1024]{2,1,0:T(8,128)(2,1)S(1)} copy-done((bf16[1,128,1024]{2,1,0:T(8,128)(2,1)S(1)}, bf16[1,128,1024]{2,1,0:T(8,128)(2,1)}, u32[]{:S(2)}) %copy-start.1) | copy-done | bytes 262168
  4.0 0.0 copy-start.2
  4.0 0.9 %copy-done.2 = bf16[1,128,1024]{2,1,0:T(8,128)(2,1)S(1)} copy-done((bf16[1,128,1024]{2,1,0:T(8,128)(2,1)S(1)}, bf16[1,128,1024]{2,1,0:T(8,128)(2,1)}, u32[]{:S(2)}) %copy-start.2) | copy-done | bytes 262168
  4.9 0.0 copy-start.3
  4.9 0.9 copy-done.3
  5.8 0.0 copy-start.5
  5.8 0.7 copy-done.5
  6.5 80.3 %shard_map.119 = (f32[1,1]{1,0:T(1,128)}, bf16[2,1024]{1,0:T(2,128)(2,1)S(1)}, bf16[128,1024]{1,0:T(8,128)(2,1)S(1)}, bf16[128,1024]{1,0:T(8,128)(2,1)S(1)}, f32[32,2048]{1,0:T(8,128)S(1)}) custom-call(bf16[128,1024]{1,0:T(8,128)(2,1)S(1)} %bitcast.11, bf16[128,1024]{1,0:T(8,128)(2,1)S(1)} %bitcast.12, bf16[2,1024]{1,0:T(2,128)(2,1)S(1)} %bitcast.15, ...), custom_call_target="tpu_custom_call" | custom-call | tf_op jit(solution)/shard_map/pallas_call | solution.py:367
  87.4 0.6 copy.19
  88.0 0.7 copy.20
  88.7 0.7 copy.21
  89.4 0.7 copy.22
  (1 shorter events, 0.0 us)
Async XLA Ops:
  0.6 0.7 copy-start.4
  0.6 0.7 copy-start.7
  1.3 0.7 copy-start.6
  2.0 1.0 %copy-start = (bf16[2048,128]{1,0:T(8,128)(2,1)S(1)}, bf16[2048,128]{1,0:T(8,128)(2,1)}, u32[]{:S(2)}) copy-start(bf16[2048,128]{1,0:T(8,128)(2,1)} %u_ref.1) | copy-start | bytes 1572868
  3.0 0.9 %copy-start.1 = (bf16[1,128,1024]{2,1,0:T(8,128)(2,1)S(1)}, bf16[1,128,1024]{2,1,0:T(8,128)(2,1)}, u32[]{:S(2)}) copy-start(bf16[1,128,1024]{2,1,0:T(8,128)(2,1)} %param.8) | copy-start | bytes 786436
  4.0 0.9 %copy-start.2 = (bf16[1,128,1024]{2,1,0:T(8,128)(2,1)S(1)}, bf16[1,128,1024]{2,1,0:T(8,128)(2,1)}, u32[]{:S(2)}) copy-start(bf16[1,128,1024]{2,1,0:T(8,128)(2,1)} %param.9) | copy-start | bytes 786436
  4.9 0.9 copy-start.3
  5.8 0.7 copy-start.5

commit v2 on v1

--- a/solution.py
+++ b/solution.py
@@ -54,10 +54,11 @@
 
 
 def kernel(
-    k_ref, v_ref, q_ref, pos_ref, tgt_ref, w_ref, gain_row_ref, gain_ref, u_ref,
-    loss_ref, gq_ref, gk_ref, gv_ref, gw_ref,
+    k_hbm, v_hbm, q_hbm, pos_hbm, tgt_hbm, w_hbm, gain_row_hbm, gain_hbm, u_hbm,
+    loss_ref, gq_ref, gk_hbm, gv_hbm, gw_ref,
+    k_ref, v_ref, q_ref, pos_ref, tgt_ref, w_ref, gain_row_ref, gain_ref, u_ref, gk_ref, gv_ref, insem,
     qsend, qbuf, wbuf, wusend, wubuf, osend, obuf, stsend, stbuf, asend, abuf, lsend, lbuf,
-    ysend, ybuf, sssend, ssbuf, dsend, dbuf, gqsend, gqbuf, gsend, gbuf, tsend, tbuf,
+    ysend, ybuf, sssend, ssbuf, dsend, dbuf, gqsend, gqbuf, gsend, gbuf, tsend, tbuf, psend, pbuf, gfull,
     s1send, s1buf, s2send, s2buf,
     flat, flat2, sc, awide, lse_s, tgt_s, own_s, kap_s, st_s,
     ssem, rsem,
@@ -66,7 +67,6 @@
     d = lax.axis_index("seq")
     y, x = d // NX, d % NX
     slab, par = d // 2, d % 2
-    owner = 16 * par + g
 
     def seq_peer(i):
         return lax.rem(d + i, NS)
@@ -84,18 +84,23 @@
         pl.semaphore_signal(barrier, inc=1, device_id={"grp": grp_peer(i), "seq": d}, device_id_type=MESH)
         return c
 
-    def greet_tiles(i, c):
-        gs, ds = d % 16, 2 * i + d // 16
-
-        @pl.when(jnp.logical_or(gs != g, ds != d))
-        def _():
-            pl.semaphore_signal(barrier, inc=1, device_id={"grp": gs, "seq": ds}, device_id_type=MESH)
-
-        return c
-
     lax.fori_loop(1, NS, greet_seq, 0)
     lax.fori_loop(1, NG, greet_grp, 0)
-    lax.fori_loop(0, SLABS, greet_tiles, 0)
+
+    def load(n, src, dst):
+        copy = pltpu.make_async_copy(src, dst, insem.at[n])
+        copy.start()
+        return copy
+
+    q_in = load(0, q_hbm, q_ref)
+    pos_in = load(1, pos_hbm, pos_ref)
+    k_in = load(2, k_hbm, k_ref)
+    v_in = load(3, v_hbm, v_ref)
+    w_in = load(4, w_hbm, w_ref)
+    u_in = load(5, u_hbm, u_ref)
+    row_in = load(6, gain_row_hbm, gain_row_ref)
+    gain_in = load(7, gain_hbm, gain_ref)
+    tgt_in = load(8, tgt_hbm, tgt_ref)
 
     def to_seq(src, dst, n):
         def one(i, c):
@@ -119,14 +124,28 @@
 
         lax.fori_loop(1, NG, one, 0)
 
+    q_in.wait()
     q32 = q_ref[...].astype(F32)
     for h in range(HEADS):
         own_s[pl.ds(h, 2, stride=8), :] = q32[:, h * HD : (h + 1) * HD]
     qsend[...] = own_s[...].astype(BF)
     qbuf[d] = own_s[...].astype(BF)
-    pos = row_to_column(pos_ref[...].astype(F32), NL)
+    pos_in.wait()
+    pos_wide = jnp.broadcast_to(pos_ref[...].astype(F32), (NL, NL))
+    pos = jnp.sum(
+        jnp.where(iota((NL, NL), 0) == iota((NL, NL), 1), pos_wide, 0.0), axis=1, keepdims=True
+    )
     places = (d * TOK + iota((NL, TOK), 1)).astype(F32)
     visible = places <= pos
+
+    pl.semaphore_wait(barrier, NS - 1 + NG - 1)
+    to_seq(lambda t: qsend, qbuf.at[d], 0)
+
+    w_in.wait()
+    u_in.wait()
+    row_in.wait()
+    gain_in.wait()
+    tgt_in.wait()
     wg = w_ref[...].astype(F32) * gain_row_ref[...]
     wg_high = wg.astype(BF)
     wg_low = (wg - wg_high.astype(F32)).astype(BF)
@@ -134,12 +153,8 @@
     wusend[...] = wu_own
     wubuf[d] = wu_own
     wbuf[d] = w_ref[:, pl.ds(pl.multiple_of(slab * 128, 128), 128)]
-
-    tiles_out = jnp.where(owner == d, NG - 1, NG)
-    pl.semaphore_wait(barrier, NS - 1 + NG - 1 + tiles_out)
-
-    to_seq(lambda t: qsend, qbuf.at[d], 0)
-    to_seq(lambda t: w_ref.at[:, pl.ds(pl.multiple_of((t // 2) * 128, 128), 128)], wbuf.at[d], 1)
+    k_in.wait()
+    v_in.wait()
 
     wait_bytes(qbuf.at[pl.ds(0, NS - 1)], rsem.at[0])
     flat[...] = qbuf[...].reshape(NL * HEADS, HD).astype(F32)
@@ -166,7 +181,7 @@
     stsend[:, 3, :] = st_s[1, pl.ds(1, NS, stride=2), :]
     to_seq(lambda t: stsend.at[t], stbuf.at[d], 3)
     to_seq(lambda t: osend.at[t], obuf.at[d], 2)
-    to_seq(lambda t: wusend, wubuf.at[d], 4)
+    to_seq(lambda t: w_ref.at[:, pl.ds(pl.multiple_of((t // 2) * 128, 128), 128)], wbuf.at[d], 1)
     stbuf[d] = stsend[d]
     obuf[d] = osend[d]
 
@@ -181,7 +196,7 @@
         denom = jnp.sum(lr * f, axis=0, keepdims=True)
         denom = jnp.where(head_lane < HEADS, denom, 1.0)
         weights.append(jnp.transpose(f / denom)[0:HEADS, :])
-        row = jnp.where(head_lane < HEADS, best + jnp.log(denom), tgt_ref[0, r].astype(F32))
+        row = jnp.where(head_lane < HEADS, best + jnp.log(denom), tgt_ref[0:1, r : r + 1].astype(F32))
         lsend[r : r + 1, :] = row
     wait_bytes(obuf.at[pl.ds(0, NS - 1)], rsem.at[2])
     w8 = jnp.concatenate(weights, axis=0)
@@ -194,11 +209,10 @@
     lbuf[d] = lsend[...]
     to_seq(lambda t: asend, abuf.at[d], 5)
     to_seq(lambda t: lsend, lbuf.at[d], 6)
+    to_seq(lambda t: wusend, wubuf.at[d], 4)
 
     wait_bytes(wbuf.at[pl.ds(0, NS - 1)], rsem.at[1])
-    wait_bytes(wubuf.at[pl.ds(0, NS - 1)], rsem.at[4])
     wc = wbuf[...].reshape(HC, 128)
-    wu = wubuf[...].reshape(HC, 128)
     wait_bytes(abuf.at[pl.ds(0, NS - 1)], rsem.at[5])
     flat2[...] = abuf[...].reshape(NL * HEADS, HD).astype(F32)
     for h in range(HEADS):
@@ -228,6 +242,8 @@
     ysend[...] = flat2[...].reshape(NS, 16, HD).astype(BF)
     near_peers(lambda t: ysend.at[t], ybuf.at[slab], 8)
     ybuf[slab] = ysend[d]
+    wait_bytes(wubuf.at[pl.ds(0, NS - 1)], rsem.at[4])
+    wu = wubuf[...].reshape(HC, 128)
     raw = dot(a, wu)
 
     wait_bytes(lbuf.at[pl.ds(0, NS - 1)], rsem.at[6])
@@ -256,7 +272,10 @@
     dx = (inverse * gain_ref[pl.ds(slab, 1), :] * dn - kappa * xs).astype(BF)
     a_half = awide[:, pl.ds(pl.multiple_of(par * 512, 512), 512)]
     gpart = dot(a_half, dx, ((0,), (0,)))
-    gsend[...] = gpart.reshape(NG, 32, 128).astype(BF)
+    gfull[...] = gpart
+    for i in range(NG):
+        for r in range(2):
+            gsend[i, r * 16 : (r + 1) * 16, :] = gfull[pl.ds(2 * i + r, 16, stride=32), :].astype(BF)
     to_grp(lambda t: gsend.at[t], gbuf.at[g], 9)
     gbuf[g] = gsend[g]
 
@@ -298,23 +317,26 @@
     s1send[...] = s1
     s1buf[d] = s1
     to_seq(lambda t: s1send, s1buf.at[d], 12)
-    tsend[...] = tile.astype(BF)
-
-    def one_owner(i, c):
-        @pl.when(jnp.logical_or(i > 0, owner != d))
+    for r in range(2):
+        tsend[:, r, :] = tile[r * 16 : (r + 1) * 16, :]
+    half = d // 16
+    first = d - 16 * par
+
+    def one_tile(i, c):
+        @pl.when(i != first)
         def _():
             pltpu.make_async_remote_copy(
-                src_ref=tsend, dst_ref=tbuf.at[slab], send_sem=ssem.at[13], recv_sem=rsem.at[13],
-                device_id={"grp": grp_peer(i), "seq": owner}, device_id_type=MESH,
+                src_ref=tsend.at[i], dst_ref=tbuf.at[slab], send_sem=ssem.at[13], recv_sem=rsem.at[13],
+                device_id={"grp": g, "seq": 16 * par + i}, device_id_type=MESH,
             ).start()
 
         return c
 
-    lax.fori_loop(0, NG, one_owner, 0)
-
-    @pl.when(owner == d)
+    lax.fori_loop(0, SLABS, one_tile, 0)
+
+    @pl.when(half == par)
     def _():
-        tbuf[slab] = tsend[...]
+        tbuf[slab] = tsend[first]
 
     for h in range(HEADS):
         cols = slice(h * HD, (h + 1) * HD)
@@ -323,45 +345,69 @@
         qh = flat[pl.ds(h, NL, stride=8), :].astype(BF)
         gk_ref[:, cols] = (dot(ds, qh, ((0,), (0,))) * SCALE).astype(BF)
 
+    gk_out = load(9, gk_ref, gk_hbm)
+    gv_out = load(10, gv_ref, gv_hbm)
     wait_bytes(s1buf.at[pl.ds(0, NS - 1)], rsem.at[12])
     s2 = jnp.sum(s1buf[:, 0, :], axis=0, keepdims=True)
     s2send[...] = s2
     s2buf[g] = s2
     to_grp(lambda t: s2send, s2buf.at[g], 14)
 
-    wait_bytes(gqbuf.at[pl.ds(0, NS - 1)], rsem.at[11])
-    own_s[...] = jnp.sum(gqbuf[...].astype(F32), axis=0)
-    for h in range(HEADS):
-        gq_ref[:, h * HD : (h + 1) * HD] = own_s[pl.ds(h, 2, stride=8), :].astype(BF)
-
-    @pl.when(owner == d)
+    @pl.when(half == par)
     def _():
         wait_bytes(tbuf.at[pl.ds(0, SLABS - 1)], rsem.at[13])
-        wait_bytes(tbuf.at[pl.ds(0, NG - 1)], ssem.at[13])
-
-    @pl.when(owner != d)
+        wait_bytes(tbuf.at[pl.ds(0, SLABS - 1)], ssem.at[13])
+
+    @pl.when(half != par)
     def _():
         wait_bytes(tbuf, rsem.at[13])
         wait_bytes(tbuf, ssem.at[13])
 
+    for r in range(2):
+        psend[r * 16 : (r + 1) * 16, :] = tbuf[:, r, :].astype(BF)
+    to_grp(lambda t: psend, pbuf.at[g], 15)
+    pbuf[g] = psend[...]
+
+    wait_bytes(gqbuf.at[pl.ds(0, NS - 1)], rsem.at[11])
+    own_s[...] = jnp.sum(gqbuf[...].astype(F32), axis=0)
+    for h in range(HEADS):
+        gq_ref[:, h * HD : (h + 1) * HD] = own_s[pl.ds(h, 2, stride=8), :].astype(BF)
+
     wait_bytes(s2buf.at[pl.ds(0, NG - 1)], rsem.at[14])
     total_squares = jnp.sum(s2buf[:, 0, :], axis=0, keepdims=True)
     factor = lax.rsqrt(total_squares * (1.0 / (HC * D)) + EPS)
+    wait_bytes(pbuf.at[pl.ds(0, NG - 1)], rsem.at[15])
+    gfull[...] = pbuf[...].reshape(NG * 32, 128).astype(F32)
     for j in range(SLABS):
-        gw_ref[:, j * 128 : (j + 1) * 128] = tbuf[j].astype(F32) * factor
-
+        gw_ref[:, j * 128 : (j + 1) * 128] = gfull[pl.ds(j, 32, stride=16), :] * factor
+
+    gk_out.wait()
+    gv_out.wait()
     for n, ref, count in (
         (0, qbuf, NS - 1), (1, wbuf, NS - 1), (2, obuf, NS - 1), (3, stbuf, NS - 1), (4, wubuf, NS - 1),
         (5, abuf, NS - 1), (6, lbuf, NS - 1), (7, ssbuf, SLABS - 1), (8, ybuf, SLABS - 1), (9, gbuf, NG - 1),
         (10, dbuf, NS - 1), (11, gqbuf, NS - 1), (12, s1buf, NS - 1), (14, s2buf, NG - 1),
+        (15, pbuf, NG - 1),
     ):
         wait_bytes(ref.at[pl.ds(0, count)], ssem.at[n])
 
 
+def write_out(loss, gq, gk, gv, gw, loss_out, gq_out, gk_out, gv_out, gw_out, l_v, q_v, k_v, v_v, w_v, sem_in, sem_out):
+    steps = ((gw, w_v, gw_out), (gk, k_v, gk_out), (gv, v_v, gv_out), (gq, q_v, gq_out), (loss, l_v, loss_out))
+    arriving = [pltpu.make_async_copy(a, m, sem_in.at[n]) for n, (a, m, b) in enumerate(steps)]
+    leaving = [pltpu.make_async_copy(m, b, sem_out.at[n]) for n, (a, m, b) in enumerate(steps)]
+    for copy in arriving:
+        copy.start()
+    for one, other in zip(arriving, leaving):
+        one.wait()
+        other.start()
+    for copy in leaving:
+        copy.wait()
+
+
 def body(hist_keys, hist_values, latent_queries, latent_pos, targets, out_proj, norm_gain, unembed):
     vmem = pl.BlockSpec(memory_space=pltpu.VMEM)
-    smem = pl.BlockSpec(memory_space=pltpu.SMEM)
-    pos = jnp.pad(latent_pos, ((0, 0), (0, 128 - NL)))
+    hbm = pl.BlockSpec(memory_space=pltpu.HBM)
     rows16 = lambda n: pltpu.VMEM((n, 16, 128), BF)
     rows32 = lambda n: pltpu.VMEM((n, 32, 128), BF)
     loss, gq, gk, gv, gw = pl.pallas_call(
@@ -373,9 +419,13 @@
             jax.ShapeDtypeStruct((TOK, HC), BF),
             jax.ShapeDtypeStruct((32, D), F32),
         ),
-        in_specs=[vmem, vmem, vmem, vmem, smem, vmem, vmem, vmem, vmem],
-        out_specs=(vmem,) * 5,
+        in_specs=[hbm] * 9,
+        out_specs=(vmem, vmem, hbm, hbm, vmem),
         scratch_shapes=[
+            pltpu.VMEM((TOK, HC), BF), pltpu.VMEM((TOK, HC), BF), pltpu.VMEM((2, HC), BF),
+            pltpu.VMEM((1, NL), jnp.int32), pltpu.VMEM((1, 2), jnp.int32), pltpu.VMEM((32, D), BF),
+            pltpu.VMEM((1, D), F32), pltpu.VMEM((SLABS, 128), F32), pltpu.VMEM((D, 128), BF),
+            pltpu.VMEM((TOK, HC), BF), pltpu.VMEM((TOK, HC), BF), pltpu.SemaphoreType.DMA((11,)),
             pltpu.VMEM((16, 128), BF), rows16(NS),
             rows32(NS), pltpu.VMEM((32, 128), BF), rows32(NS),
             rows16(NS), rows16(NS),
@@ -387,7 +437,8 @@
             pltpu.VMEM((16, 128), BF), rows16(NS),
             rows16(NS), rows16(NS),
             rows32(NG), rows32(NG),
-            pltpu.VMEM((32, 128), BF), rows32(SLABS),
+            pltpu.VMEM((SLABS, 2, 128), F32), pltpu.VMEM((SLABS, 2, 128), F32),
+            pltpu.VMEM((32, 128), BF), rows32(NG), pltpu.VMEM((512, 128), F32),
             pltpu.VMEM((1, 128), F32), pltpu.VMEM((NS, 1, 128), F32),
             pltpu.VMEM((1, 128), F32), pltpu.VMEM((NG, 1, 128), F32),
             pltpu.VMEM((NL * HEADS, 128), F32), pltpu.VMEM((NL * HEADS, 128), F32),
@@ -396,15 +447,33 @@
             pltpu.VMEM((HEADS, NL, 128), F32), pltpu.VMEM((NL, 128), F32),
             pltpu.VMEM((16, 128), F32), pltpu.VMEM((NL, 128), F32),
             pltpu.VMEM((2, NL, 128), F32),
-            pltpu.SemaphoreType.DMA((15,)), pltpu.SemaphoreType.DMA((15,)),
+            pltpu.SemaphoreType.DMA((16,)), pltpu.SemaphoreType.DMA((16,)),
         ],
         compiler_params=pltpu.CompilerParams(
-            collective_id=0, has_side_effects=True, vmem_limit_bytes=32 << 20
+            collective_id=0, has_side_effects=True, vmem_limit_bytes=56 << 20
         ),
     )(
-        hist_keys[0], hist_values[0], latent_queries[0], pos, targets, out_proj,
+        hist_keys[0], hist_values[0], latent_queries[0], latent_pos, targets, out_proj,
         norm_gain.reshape(1, D), norm_gain.reshape(SLABS, 128), unembed,
     )
+    loss, gq, gk, gv, gw = pl.pallas_call(
+        write_out,
+        out_shape=(
+            jax.ShapeDtypeStruct((1, 1), F32),
+            jax.ShapeDtypeStruct((2, HC), BF),
+            jax.ShapeDtypeStruct((TOK, HC), BF),
+            jax.ShapeDtypeStruct((TOK, HC), BF),
+            jax.ShapeDtypeStruct((32, D), F32),
+        ),
+        in_specs=[hbm] * 5,
+        out_specs=(hbm,) * 5,
+        scratch_shapes=[
+            pltpu.VMEM((1, 1), F32), pltpu.VMEM((2, HC), BF), pltpu.VMEM((TOK, HC), BF),
+            pltpu.VMEM((TOK, HC), BF), pltpu.VMEM((32, D), F32),
+            pltpu.SemaphoreType.DMA((5,)), pltpu.SemaphoreType.DMA((5,)),
+        ],
+        compiler_params=pltpu.CompilerParams(vmem_limit_bytes=56 << 20),
+    )(loss, gq, gk, gv, gw)
     return loss.reshape(1), gq[None], gk[None], gv[None], gw
 
 

time: 91.6 us -> 76.3 us (0.83)
  local copies, waits for them, and re-layouts: 8.54 us -> 0 us
  Pallas kernels: 80.3 us -> 75.5 us
  between operations: 2.47 us -> 0.64 us
    unnamed x20 -> x0, local copies, waits for them, and re-layouts: 8.54 us -> none
    pallas_call x1, Pallas kernels: 80.3 us -> 73 us  [body(): pl.pallas_call(kernel, out_shape=(jax.ShapeDtypeStruct((1, 1), F32), jax....]
    pallas_call x0 -> x1, Pallas kernels: none -> 2.54 us  [body(): pl.pallas_call(write_out, out_shape=(jax.ShapeDtypeStruct((1, 1), F32), j...]
where the time goes in v2:
time: 76.3 us; the launch traced here: 76.1 us
  Pallas kernels  75.5 us (99%)
    pallas_call x1, Pallas kernels, body(): pl.pallas_call(kernel, out_shape=(jax.ShapeDtypeStruct((1, 1), F32), jax....  73 us
    pallas_call x1, Pallas kernels, body(): pl.pallas_call(write_out, out_shape=(jax.ShapeDtypeStruct((1, 1), F32), j...  2.54 us

profile of v2, /device:TPU:1, one launch (start us, length us, event | category | flops | bytes accessed | tf_op | source)
XLA Modules:
  0.0 76.1 jit_solution(13691903250767570002)
XLA Ops:
  0.6 73.0 %shard_map.119 = (f32[1,1]{1,0:T(1,128)}, bf16[2,1024]{1,0:T(2,128)(2,1)}, bf16[128,1024]{1,0:T(8,128)(2,1)}, bf16[128,1024]{1,0:T(8,128)(2,1)}, f32[32,2048]{1,0:T(8,128)}) custom-call(bf16[128,1024]{1,0:T(8,128)(2,1)} %bitcast.9, bf16[128,1024]{1,0:T(8,128)(2,1)} %bitcast.10, bf16[2,1024]{1,0:T(2,128)(2,1)} %bitcast.13, s32[1,64]{1,0:T(1,128)} %pos_hbm.1, ...), custom_call_target="tpu_custom_call" | custom-call | tf_op jit(solution)/shard_map/pallas_call | solution.py:413
  73.6 2.5 %shard_map.120 = (f32[1,1]{1,0:T(1,128)}, bf16[2,1024]{1,0:T(2,128)(2,1)}, bf16[128,1024]{1,0:T(8,128)(2,1)}, bf16[128,1024]{1,0:T(8,128)(2,1)}, f32[32,2048]{1,0:T(8,128)}) custom-call(f32[1,1]{1,0:T(1,128)} %get-tuple-element.15.loss, bf16[2,1024]{1,0:T(2,128)(2,1)} %get-tuple-element.16.gq, bf16[128,1024]{1,0:T(8,128)(2,1)} %get-tuple-element.17.gk, ...), custom_call_target="tpu_custom_call" | custom-call | tf_op jit(solution)/shard_map/pallas_call | solution.py:459

commit v3 on v2

--- a/solution.py
+++ b/solution.py
@@ -68,11 +68,14 @@
     y, x = d // NX, d % NX
     slab, par = d // 2, d % 2
 
+    def spread(i, middle):
+        return middle + jnp.where(i % 2 == 0, i // 2, -((i + 1) // 2))
+
     def seq_peer(i):
-        return lax.rem(d + i, NS)
+        return lax.rem(y + spread(i // NX, NY // 2), NY) * NX + lax.rem(x + spread(i % NX, NX // 2), NX)
 
     def grp_peer(i):
-        return lax.rem(g + i, NG)
+        return lax.rem(g // 2 + spread(i // 2, 4), NG // 2) * 2 + lax.rem(g + 1 + i, 2)
 
     barrier = pltpu.get_barrier_semaphore()
 
@@ -84,8 +87,8 @@
         pl.semaphore_signal(barrier, inc=1, device_id={"grp": grp_peer(i), "seq": d}, device_id_type=MESH)
         return c
 
-    lax.fori_loop(1, NS, greet_seq, 0)
-    lax.fori_loop(1, NG, greet_grp, 0)
+    lax.fori_loop(0, NS - 1, greet_seq, 0)
+    lax.fori_loop(0, NG - 1, greet_grp, 0)
 
     def load(n, src, dst):
         copy = pltpu.make_async_copy(src, dst, insem.at[n])
@@ -102,16 +105,17 @@
     gain_in = load(7, gain_hbm, gain_ref)
     tgt_in = load(8, tgt_hbm, tgt_ref)
 
-    def to_seq(src, dst, n):
+    def to_seq(*sends):
         def one(i, c):
             t = seq_peer(i)
-            pltpu.make_async_remote_copy(
-                src_ref=src(t), dst_ref=dst, send_sem=ssem.at[n], recv_sem=rsem.at[n],
-                device_id={"grp": g, "seq": t}, device_id_type=MESH,
-            ).start()
+            for src, dst, n in sends:
+                pltpu.make_async_remote_copy(
+                    src_ref=src(t), dst_ref=dst, send_sem=ssem.at[n], recv_sem=rsem.at[n],
+                    device_id={"grp": g, "seq": t}, device_id_type=MESH,
+                ).start()
             return c
 
-        lax.fori_loop(1, NS, one, 0)
+        lax.fori_loop(0, NS - 1, one, 0, unroll=True)
 
     def to_grp(src, dst, n):
         def one(i, c):
@@ -122,7 +126,7 @@
             ).start()
             return c
 
-        lax.fori_loop(1, NG, one, 0)
+        lax.fori_loop(0, NG - 1, one, 0, unroll=True)
 
     q_in.wait()
     q32 = q_ref[...].astype(F32)
@@ -137,9 +141,6 @@
     )
     places = (d * TOK + iota((NL, TOK), 1)).astype(F32)
     visible = places <= pos
-
-    pl.semaphore_wait(barrier, NS - 1 + NG - 1)
-    to_seq(lambda t: qsend, qbuf.at[d], 0)
 
     w_in.wait()
     u_in.wait()
@@ -155,6 +156,10 @@
     wbuf[d] = w_ref[:, pl.ds(pl.multiple_of(slab * 128, 128), 128)]
     k_in.wait()
     v_in.wait()
+
+    pl.semaphore_wait(barrier, NS - 1 + NG - 1)
+    to_seq((lambda t: qsend, qbuf.at[d], 0))
+    to_seq((lambda t: w_ref.at[:, pl.ds(pl.multiple_of((t // 2) * 128, 128), 128)], wbuf.at[d], 1))
 
     wait_bytes(qbuf.at[pl.ds(0, NS - 1)], rsem.at[0])
     flat[...] = qbuf[...].reshape(NL * HEADS, HD).astype(F32)
@@ -179,9 +184,8 @@
     stsend[:, 1, :] = st_s[0, pl.ds(1, NS, stride=2), :]
     stsend[:, 2, :] = st_s[1, pl.ds(0, NS, stride=2), :]
     stsend[:, 3, :] = st_s[1, pl.ds(1, NS, stride=2), :]
-    to_seq(lambda t: stsend.at[t], stbuf.at[d], 3)
-    to_seq(lambda t: osend.at[t], obuf.at[d], 2)
-    to_seq(lambda t: w_ref.at[:, pl.ds(pl.multiple_of((t // 2) * 128, 128), 128)], wbuf.at[d], 1)
+    to_seq((lambda t: stsend.at[t], stbuf.at[d], 3), (lambda t: osend.at[t], obuf.at[d], 2))
+    to_seq((lambda t: wusend, wubuf.at[d], 4))
     stbuf[d] = stsend[d]
     obuf[d] = osend[d]
 
@@ -207,9 +211,7 @@
     asend[...] = attn_own
     abuf[d] = attn_own
     lbuf[d] = lsend[...]
-    to_seq(lambda t: asend, abuf.at[d], 5)
-    to_seq(lambda t: lsend, lbuf.at[d], 6)
-    to_seq(lambda t: wusend, wubuf.at[d], 4)
+    to_seq((lambda t: asend, abuf.at[d], 5), (lambda t: lsend, lbuf.at[d], 6))
 
     wait_bytes(wbuf.at[pl.ds(0, NS - 1)], rsem.at[1])
     wc = wbuf[...].reshape(HC, 128)
@@ -225,15 +227,15 @@
 
     def near_peers(src, dst, n):
         def one(i, c):
-            tx = jnp.where(i % 2 == 0, x, NX - 1 - x)
-            t = lax.rem(y + i // 2, NY) * NX + tx
+            tx = jnp.where(i % 2 == 0, NX - 1 - x, x)
+            t = lax.rem(y + spread(i // 2, NY // 2), NY) * NX + tx
             pltpu.make_async_remote_copy(
                 src_ref=src(t), dst_ref=dst, send_sem=ssem.at[n], recv_sem=rsem.at[n],
                 device_id={"grp": g, "seq": t}, device_id_type=MESH,
             ).start()
             return c
 
-        lax.fori_loop(1, SLABS, one, 0)
+        lax.fori_loop(0, SLABS - 1, one, 0, unroll=True)
 
     near_peers(lambda t: sssend, ssbuf.at[slab], 7)
     xb = xs.astype(BF)
@@ -289,7 +291,7 @@
     dattn_own = (flat2[pl.ds(pl.multiple_of(d * 16, 16), 16), :] - k2 * ysum).astype(BF)
     dsend[...] = dattn_own
     dbuf[d] = dattn_own
-    to_seq(lambda t: dsend, dbuf.at[d], 10)
+    to_seq((lambda t: dsend, dbuf.at[d], 10))
 
     wait_bytes(dbuf.at[pl.ds(0, NS - 1)], rsem.at[10])
     flat2[...] = dbuf[...].reshape(NL * HEADS, HD).astype(F32)
@@ -307,7 +309,7 @@
         cols = slice(h * HD, (h + 1) * HD)
         flat2[pl.ds(h, NL, stride=8), :] = dot(kept[h][1], k_ref[:, cols]) * SCALE
     gqsend[...] = flat2[...].reshape(NS, 16, HD).astype(BF)
-    to_seq(lambda t: gqsend.at[t], gqbuf.at[d], 11)
+    to_seq((lambda t: gqsend.at[t], gqbuf.at[d], 11))
     gqbuf[d] = gqsend[d]
 
     wait_bytes(gbuf.at[pl.ds(0, NG - 1)], rsem.at[9])
@@ -316,7 +318,7 @@
     s1 = jnp.broadcast_to(squares, (1, 128))
     s1send[...] = s1
     s1buf[d] = s1
-    to_seq(lambda t: s1send, s1buf.at[d], 12)
+    to_seq((lambda t: s1send, s1buf.at[d], 12))
     for r in range(2):
         tsend[:, r, :] = tile[r * 16 : (r + 1) * 16, :]
     half = d // 16

time: 76.3 us -> 71 us (0.931)
  Pallas kernels: 75.5 us -> 70.2 us
    pallas_call x1, Pallas kernels: 73 us -> 67.6 us  [body(): pl.pallas_call(kernel, out_shape=(jax.ShapeDtypeStruct((1, 1), F32), jax....]
where the time goes in v3:
time: 71 us; the launch traced here: 70.8 us
  Pallas kernels  70.2 us (99%)
    pallas_call x1, Pallas kernels, body(): pl.pallas_call(kernel, out_shape=(jax.ShapeDtypeStruct((1, 1), F32), jax....  67.6 us
    pallas_call x1, Pallas kernels, body(): pl.pallas_call(write_out, out_shape=(jax.ShapeDtypeStruct((1, 1), F32), j...  2.54 us

profile of v3, /device:TPU:1, one launch (start us, length us, event | category | flops | bytes accessed | tf_op | source)
XLA Modules:
  0.0 70.8 jit_solution(6063787449216539246)
XLA Ops:
  0.6 67.6 %shard_map.119 = (f32[1,1]{1,0:T(1,128)}, bf16[2,1024]{1,0:T(2,128)(2,1)}, bf16[128,1024]{1,0:T(8,128)(2,1)}, bf16[128,1024]{1,0:T(8,128)(2,1)}, f32[32,2048]{1,0:T(8,128)}) custom-call(bf16[128,1024]{1,0:T(8,128)(2,1)} %bitcast.9, bf16[128,1024]{1,0:T(8,128)(2,1)} %bitcast.10, bf16[2,1024]{1,0:T(2,128)(2,1)} %bitcast.13, s32[1,64]{1,0:T(1,128)} %pos_hbm.1, ...), custom_call_target="tpu_custom_call" | custom-call | tf_op jit(solution)/shard_map/pallas_call | solution.py:415
  68.3 2.5 %shard_map.120 = (f32[1,1]{1,0:T(1,128)}, bf16[2,1024]{1,0:T(2,128)(2,1)}, bf16[128,1024]{1,0:T(8,128)(2,1)}, bf16[128,1024]{1,0:T(8,128)(2,1)}, f32[32,2048]{1,0:T(8,128)}) custom-call(f32[1,1]{1,0:T(1,128)} %get-tuple-element.15.loss, bf16[2,1024]{1,0:T(2,128)(2,1)} %get-tuple-element.16.gq, bf16[128,1024]{1,0:T(8,128)(2,1)} %get-tuple-element.17.gk, ...), custom_call_target="tpu_custom_call" | custom-call | tf_op jit(solution)/shard_map/pallas_call | solution.py:461

commit v4 on v3

--- a/solution.py
+++ b/solution.py
@@ -185,7 +185,6 @@
     stsend[:, 2, :] = st_s[1, pl.ds(0, NS, stride=2), :]
     stsend[:, 3, :] = st_s[1, pl.ds(1, NS, stride=2), :]
     to_seq((lambda t: stsend.at[t], stbuf.at[d], 3), (lambda t: osend.at[t], obuf.at[d], 2))
-    to_seq((lambda t: wusend, wubuf.at[d], 4))
     stbuf[d] = stsend[d]
     obuf[d] = osend[d]
 
@@ -212,6 +211,7 @@
     abuf[d] = attn_own
     lbuf[d] = lsend[...]
     to_seq((lambda t: asend, abuf.at[d], 5), (lambda t: lsend, lbuf.at[d], 6))
+    to_seq((lambda t: wusend, wubuf.at[d], 4))
 
     wait_bytes(wbuf.at[pl.ds(0, NS - 1)], rsem.at[1])
     wc = wbuf[...].reshape(HC, 128)
@@ -293,25 +293,6 @@
     dbuf[d] = dattn_own
     to_seq((lambda t: dsend, dbuf.at[d], 10))
 
-    wait_bytes(dbuf.at[pl.ds(0, NS - 1)], rsem.at[10])
-    flat2[...] = dbuf[...].reshape(NL * HEADS, HD).astype(F32)
-    kept = []
-    for h in range(HEADS):
-        cols = slice(h * HD, (h + 1) * HD)
-        d32 = flat2[pl.ds(h, NL, stride=8), :]
-        dh = d32.astype(BF)
-        delta = jnp.sum(d32 * awide[:, cols].astype(F32), axis=-1, keepdims=True)
-        probs = jnp.where(visible, jnp.exp(sc[h] - lse_s[h]), 0.0)
-        dp = dot(dh, v_ref[:, cols], RANGE_T)
-        ds = (probs * (dp - delta)).astype(BF)
-        kept.append((probs.astype(BF), ds, dh))
-    for h in range(HEADS):
-        cols = slice(h * HD, (h + 1) * HD)
-        flat2[pl.ds(h, NL, stride=8), :] = dot(kept[h][1], k_ref[:, cols]) * SCALE
-    gqsend[...] = flat2[...].reshape(NS, 16, HD).astype(BF)
-    to_seq((lambda t: gqsend.at[t], gqbuf.at[d], 11))
-    gqbuf[d] = gqsend[d]
-
     wait_bytes(gbuf.at[pl.ds(0, NG - 1)], rsem.at[9])
     tile = jnp.sum(gbuf[...].astype(F32), axis=0)
     squares = jnp.sum(jnp.sum(tile * tile, axis=0, keepdims=True), axis=1, keepdims=True)
@@ -340,6 +321,46 @@
     def _():
         tbuf[slab] = tsend[first]
 
+    wait_bytes(dbuf.at[pl.ds(0, NS - 1)], rsem.at[10])
+    flat2[...] = dbuf[...].reshape(NL * HEADS, HD).astype(F32)
+    kept = []
+    for h in range(HEADS):
+        cols = slice(h * HD, (h + 1) * HD)
+        d32 = flat2[pl.ds(h, NL, stride=8), :]
+        dh = d32.astype(BF)
+        delta = jnp.sum(d32 * awide[:, cols].astype(F32), axis=-1, keepdims=True)
+        probs = jnp.where(visible, jnp.exp(sc[h] - lse_s[h]), 0.0)
+        dp = dot(dh, v_ref[:, cols], RANGE_T)
+        ds = (probs * (dp - delta)).astype(BF)
+        kept.append((probs.astype(BF), ds, dh))
+    for h in range(HEADS):
+        cols = slice(h * HD, (h + 1) * HD)
+        flat2[pl.ds(h, NL, stride=8), :] = dot(kept[h][1], k_ref[:, cols]) * SCALE
+    gqsend[...] = flat2[...].reshape(NS, 16, HD).astype(BF)
+    to_seq((lambda t: gqsend.at[t], gqbuf.at[d], 11))
+    gqbuf[d] = gqsend[d]
+
+    wait_bytes(s1buf.at[pl.ds(0, NS - 1)], rsem.at[12])
+    s2 = jnp.sum(s1buf[:, 0, :], axis=0, keepdims=True)
+    s2send[...] = s2
+    s2buf[g] = s2
+    to_grp(lambda t: s2send, s2buf.at[g], 14)
+
+    @pl.when(half == par)
+    def _():
+        wait_bytes(tbuf.at[pl.ds(0, SLABS - 1)], rsem.at[13])
+        wait_bytes(tbuf.at[pl.ds(0, SLABS - 1)], ssem.at[13])
+
+    @pl.when(half != par)
+    def _():
+        wait_bytes(tbuf, rsem.at[13])
+        wait_bytes(tbuf, ssem.at[13])
+
+    for r in range(2):
+        psend[r * 16 : (r + 1) * 16, :] = tbuf[:, r, :].astype(BF)
+    to_grp(lambda t: psend, pbuf.at[g], 15)
+    pbuf[g] = psend[...]
+
     for h in range(HEADS):
         cols = slice(h * HD, (h + 1) * HD)
         pr, ds, dh = kept[h]
@@ -349,26 +370,6 @@
 
     gk_out = load(9, gk_ref, gk_hbm)
     gv_out = load(10, gv_ref, gv_hbm)
-    wait_bytes(s1buf.at[pl.ds(0, NS - 1)], rsem.at[12])
-    s2 = jnp.sum(s1buf[:, 0, :], axis=0, keepdims=True)
-    s2send[...] = s2
-    s2buf[g] = s2
-    to_grp(lambda t: s2send, s2buf.at[g], 14)
-
-    @pl.when(half == par)
-    def _():
-        wait_bytes(tbuf.at[pl.ds(0, SLABS - 1)], rsem.at[13])
-        wait_bytes(tbuf.at[pl.ds(0, SLABS - 1)], ssem.at[13])
-
-    @pl.when(half != par)
-    def _():
-        wait_bytes(tbuf, rsem.at[13])
-        wait_bytes(tbuf, ssem.at[13])
-
-    for r in range(2):
-        psend[r * 16 : (r + 1) * 16, :] = tbuf[:, r, :].astype(BF)
-    to_grp(lambda t: psend, pbuf.at[g], 15)
-    pbuf[g] = psend[...]
 
     wait_bytes(gqbuf.at[pl.ds(0, NS - 1)], rsem.at[11])
     own_s[...] = jnp.sum(gqbuf[...].astype(F32), axis=0)

time: 71 us -> 67.9 us (0.956)
  Pallas kernels: 70.2 us -> 67.1 us
    pallas_call x1, Pallas kernels: 67.6 us -> 64.6 us  [body(): pl.pallas_call(kernel, out_shape=(jax.ShapeDtypeStruct((1, 1), F32), jax....]
where the time goes in v4:
time: 67.9 us; the launch traced here: 67.8 us
  Pallas kernels  67.1 us (99%)
    pallas_call x1, Pallas kernels, body(): pl.pallas_call(kernel, out_shape=(jax.ShapeDtypeStruct((1, 1), F32), jax....  64.6 us
    pallas_call x1, Pallas kernels, body(): pl.pallas_call(write_out, out_shape=(jax.ShapeDtypeStruct((1, 1), F32), j...  2.54 us

profile of v4, /device:TPU:1, one launch (start us, length us, event | category | flops | bytes accessed | tf_op | source)
XLA Modules:
  0.0 67.8 jit_solution(4720558914820597137)
XLA Ops:
  0.6 64.6 %shard_map.119 = (f32[1,1]{1,0:T(1,128)}, bf16[2,1024]{1,0:T(2,128)(2,1)}, bf16[128,1024]{1,0:T(8,128)(2,1)}, bf16[128,1024]{1,0:T(8,128)(2,1)}, f32[32,2048]{1,0:T(8,128)}) custom-call(bf16[128,1024]{1,0:T(8,128)(2,1)} %bitcast.9, bf16[128,1024]{1,0:T(8,128)(2,1)} %bitcast.10, bf16[2,1024]{1,0:T(2,128)(2,1)} %bitcast.13, s32[1,64]{1,0:T(1,128)} %pos_hbm.1, ...), custom_call_target="tpu_custom_call" | custom-call | tf_op jit(solution)/shard_map/pallas_call | solution.py:416
  65.2 2.5 %shard_map.120 = (f32[1,1]{1,0:T(1,128)}, bf16[2,1024]{1,0:T(2,128)(2,1)}, bf16[128,1024]{1,0:T(8,128)(2,1)}, bf16[128,1024]{1,0:T(8,128)(2,1)}, f32[32,2048]{1,0:T(8,128)}) custom-call(f32[1,1]{1,0:T(1,128)} %get-tuple-element.15.loss, bf16[2,1024]{1,0:T(2,128)(2,1)} %get-tuple-element.16.gq, bf16[128,1024]{1,0:T(8,128)(2,1)} %get-tuple-element.17.gk, ...), custom_call_target="tpu_custom_call" | custom-call | tf_op jit(solution)/shard_map/pallas_call | solution.py:462
